TPU v7x, 32 devices: a whole 2x2x4 slice. The times are simulated.
32 devices in a mesh: harm: 4 (over z), node: 8 (over y, x, core).
Axes of the slice: x: 2, y: 2, z: 4, core: 2. Of those that a mesh axis runs over, the one named last changes fastest.
Arguments:
- adjoint: bfloat16 [128, 4, 32768], P('harm', None, 'node'), may hold values from -6 to 6
- source: float32 [128, 131072], P(None, ('harm', 'node')), may hold values from -6 to 6
- rad_coeff: bfloat16 [128, 131072], P(None, ('harm', 'node')), may hold values from 0.19921875 to 2
- capacity: float32 [131072], P(('harm', 'node')), may hold values from 0.005 to 0.03
- inv_diag: float32 [131072], P(('harm', 'node')), may hold values from 0.1 to 0.5
- blocks: bfloat16 [1024, 4, 128, 128], P(('harm', 'node')), may hold values from -0.25 to 0.25
- block_cols: int32 [1024, 4], P(('harm', 'node')), may hold values from 0 to 1023, as said below
- zone_of: int32 [131072], P(('harm', 'node')), may hold values from 0 to 1279, as said below
- heater_weight: float32 [131072], P(('harm', 'node')), may hold values from 0.2 to 2
Outputs:
- updated: bfloat16 [128, 4, 32768], P('harm', None, 'node')
- gradient: float32 [1280, 128], P(('harm', 'node'))
Inputs may be any that keep to these rules, and one draw needn't show every extreme that they name: `block_cols`: with d = b // 32 and D = 32: slot 0 of row block b names b itself; slot 1 lies in row blocks max(d - 1, 0) * 32 to (max(d - 1, 0) + 1) * 32 - 1; slot 2 in min(d + 1, D - 1) * 32 to (min(d + 1, D - 1) + 1) * 32 - 1; the other slots in (d - 1) * 32 to (d + 2) * 32 - 1. `zone_of`: node n lies in a zone z with (n // 4096 - 1) * 40 <= z < (n // 4096 + 2) * 40.
All inputs are finite; a program needn't handle non-finite values.
Results may differ from a plain program's by a relative error of at most 0.0035.
Values may be sent and summed in bfloat16 or wider, within the bound.
A program may use at most 64 MiB of HBM per device.

v0:
```python
import functools
import math

import jax
import jax.numpy as jnp
import numpy as np
from jax import lax
from jax.experimental import pallas as pl
from jax.experimental.pallas import tpu as pltpu
from jax.sharding import PartitionSpec as P

ZONE_DEV = 40
ROWS = 16
GROUPS = 4
WIDTH = 256
MESH = pl.DeviceIdType.MESH
NT = (((1,), (1,)), ((), ()))


def fourier_basis(count):
    sample_index = np.arange(count, dtype=np.float32)[:, None]
    column_index = np.arange(count)[None, :]
    half_count = count // 2
    frequency = np.where(
        column_index <= half_count, column_index, column_index - half_count
    ).astype(np.float32)
    angle = np.float32(2.0 * math.pi) * frequency * sample_index / np.float32(count)
    values_table = np.where(column_index <= half_count, np.cos(angle), np.sin(angle))
    scaling = np.where(
        (column_index == 0) | (column_index == half_count),
        math.sqrt(1.0 / count),
        math.sqrt(2.0 / count),
    ).astype(np.float32)
    return (values_table * scaling).astype(jnp.bfloat16)


def kernel(
    n_harm,
    n_node,
    n_chunk,
    adj,
    src_any,
    rad_any,
    blk_any,
    capacity,
    inv_diag,
    weight,
    zone,
    cols,
    fourier,
    fourier_t,
    rate_k,
    ret,
    grad,
    *scratch,
):
    ext = scratch[:n_chunk]
    (
        src,
        rad,
        blk,
        upd,
        select,
        part,
        from_prev,
        from_next,
        load_sem,
        in_send,
        in_recv,
        halo_send,
        halo_recv,
        out_send,
        out_recv,
        own_sem,
        part_send,
        part_recv,
    ) = scratch[n_chunk:]
    row_blocks = adj.shape[2]
    nodes = row_blocks * 128
    chunk_rows = n_harm * ROWS
    me_h = lax.axis_index("harm")
    me_n = lax.axis_index("node")
    pos = me_h * n_node + me_n
    last = n_harm * n_node - 1
    has_prev = pos > 0
    has_next = pos < last
    prev = jnp.maximum(pos - 1, 0)
    following = jnp.minimum(pos + 1, last)
    prev_id = (prev // n_node, prev % n_node)
    next_id = (following // n_node, following % n_node)
    sides = ((has_prev, prev_id, 2), (has_next, next_id, 0))

    loads = [
        pltpu.make_async_copy(src_any, src, load_sem.at[0]),
        pltpu.make_async_copy(rad_any, rad, load_sem.at[1]),
        pltpu.make_async_copy(blk_any, blk, load_sem.at[2]),
    ]
    own = [
        pltpu.make_async_copy(
            adj.at[me_h, c], ext[c].at[me_h, pl.ds(row_blocks, row_blocks)], load_sem.at[3 + c]
        )
        for c in range(n_chunk)
    ]

    barrier = pltpu.get_barrier_semaphore()
    for d in range(1, n_harm):
        peer = lax.rem(me_h + d, n_harm)
        pl.semaphore_signal(barrier, inc=1, device_id=(peer, me_n), device_id_type=MESH)
    for there, device, _ in sides:

        @pl.when(there)
        def _(device=device):
            pl.semaphore_signal(barrier, inc=1, device_id=device, device_id_type=MESH)

    pl.semaphore_wait(
        barrier, n_harm - 1 + has_prev.astype(jnp.int32) + has_next.astype(jnp.int32)
    )

    def arrive(d, c):
        peer = lax.rem(me_h + d, n_harm)
        return pltpu.make_async_remote_copy(
            src_ref=adj.at[peer, c],
            dst_ref=ext[c].at[me_h, pl.ds(row_blocks, row_blocks)],
            send_sem=in_send.at[d, c],
            recv_sem=in_recv.at[d, c],
            device_id=(peer, me_n),
            device_id_type=MESH,
        )

    def halo(d, c, side):
        _, device, place = sides[side]
        piece = lax.rem(me_h - d + n_harm, n_harm)
        if d == 0:
            source = adj.at[me_h, c]
        else:
            source = ext[c].at[piece, pl.ds(row_blocks, row_blocks)]
        return pltpu.make_async_remote_copy(
            src_ref=source,
            dst_ref=ext[c].at[piece, pl.ds(place * row_blocks, row_blocks)],
            send_sem=halo_send.at[side, d, c],
            recv_sem=halo_recv.at[side, d, c],
            device_id=device,
            device_id_type=MESH,
        )

    def start_halo(d, c):
        for side in range(2):

            @pl.when(sides[side][0])
            def _(side=side):
                halo(d, c, side).start()

    for c in range(n_chunk):
        for d in range(1, n_harm):
            arrive(d, c).start()
        own[c].start()
        start_halo(0, c)
    for load in loads:
        load.start()

    zone_row = lax.broadcasted_iota(jnp.int32, (128, WIDTH), 0)

    def select_step(i, carry):
        at = pl.ds(pl.multiple_of(i * WIDTH, WIDTH), WIDTH)
        hit = zone_row == (zone[:, at] - (pos - 1) * ZONE_DEV)
        w = weight[:, at]
        high = w.astype(jnp.bfloat16).astype(jnp.float32)
        select[0:128, at] = jnp.where(hit, high, 0.0).astype(jnp.bfloat16)
        select[128:256, at] = jnp.where(hit, w - high, 0.0).astype(jnp.bfloat16)
        return carry

    lax.fori_loop(0, nodes // WIDTH, select_step, 0)

    for c in range(n_chunk):
        own[c].wait()
        for d in range(1, n_harm):
            arrive(d, c).wait_recv()
            start_halo(d, c)
    for load in loads:
        load.wait()

    def block_of(c, index):
        return jnp.concatenate([ext[c][h, index] for h in range(n_harm)], axis=0)

    half = chunk_rows // 2

    def local_step(i, carry):
        at = pl.ds(pl.multiple_of(i * WIDTH, WIDTH), WIDTH)
        first = row_blocks + i * (WIDTH // 128)
        pieces = [
            jnp.concatenate([block_of(c, first + t) for t in range(WIDTH // 128)], axis=1)
            for c in range(n_chunk)
        ]
        field = jnp.concatenate(pieces, axis=0) if n_chunk > 1 else pieces[0]
        samples = jnp.dot(fourier[...], field, preferred_element_type=jnp.float32)
        weighted = (rad[:, at].astype(jnp.float32) * samples).astype(jnp.bfloat16)
        radiative = jnp.dot(fourier_t[...], weighted, preferred_element_type=jnp.float32)
        cap = capacity[:, at]
        for c in range(n_chunk):
            lam = pieces[c].astype(jnp.float32)
            swapped = jnp.concatenate([lam[half:], lam[:half]], axis=0)
            rows = slice(c * chunk_rows, (c + 1) * chunk_rows)
            rate = rate_k[rows, :] * swapped
            rest = src[:, c, :, at].reshape(chunk_rows, WIDTH) - (cap * rate + radiative[rows])
            src[:, c, :, at] = rest.reshape(n_harm, ROWS, WIDTH)
        return carry

    lax.fori_loop(0, nodes // WIDTH, local_step, 0)

    group = nodes // GROUPS
    group_blocks = group // 128

    def back(d, c, q):
        peer = lax.rem(me_h + d, n_harm)
        return pltpu.make_async_remote_copy(
            src_ref=upd.at[peer, c, :, pl.ds(q * group, group)],
            dst_ref=ret.at[me_h, c, :, pl.ds(q * group, group)],
            send_sem=out_send.at[d, c, q],
            recv_sem=out_recv.at[d, c, q],
            device_id=(peer, me_n),
            device_id_type=MESH,
        )

    def own_back(c, q):
        return pltpu.make_async_copy(
            upd.at[me_h, c, :, pl.ds(q * group, group)],
            ret.at[me_h, c, :, pl.ds(q * group, group)],
            own_sem.at[c, q],
        )

    for c in range(n_chunk):
        for side in range(2):

            @pl.when(sides[1 - side][0])
            def _(side=side, c=c):
                for d in range(n_harm):
                    halo(d, c, side).wait_recv()

        for q in range(GROUPS):

            def block_step(i, carry, c=c, q=q):
                b = q * group_blocks + i
                at = pl.ds(pl.multiple_of(b * 128, 128), 128)
                lam = block_of(c, row_blocks + b)
                taken = [lam]
                for s in range(1, blk.shape[1]):
                    col = cols[s, b] - (pos - 1) * row_blocks
                    col = jnp.minimum(jnp.maximum(col, 0), 3 * row_blocks - 1)
                    taken.append(block_of(c, col))
                conductance = jnp.concatenate(
                    [blk[b, s] for s in range(blk.shape[1])], axis=1
                )
                conduction = lax.dot_general(
                    jnp.concatenate(taken, axis=1),
                    conductance,
                    NT,
                    preferred_element_type=jnp.float32,
                )
                residual = src[:, c, :, at].reshape(chunk_rows, 128) - conduction
                new = lam.astype(jnp.float32) + inv_diag[:, at] * residual
                upd[:, c, :, at] = new.astype(jnp.bfloat16).reshape(n_harm, ROWS, 128)
                return carry

            lax.fori_loop(0, group_blocks, block_step, 0, unroll=2)
            for d in range(1, n_harm):
                back(d, c, q).start()
            own_back(c, q).start()

    part[...] = jnp.zeros_like(part)

    def gradient_step(i, carry):
        at = pl.ds(pl.multiple_of(i * 512, 512), 512)
        new = upd[:, :, :, at].reshape(n_chunk * chunk_rows, 512)
        both = lax.dot_general(select[:, at], new, NT, preferred_element_type=jnp.float32)
        part[...] += both[0:128] + both[128:256]
        return carry

    lax.fori_loop(0, nodes // 512, gradient_step, 0)

    def hand_over(side):
        _, device, place = sides[side]
        rows = pl.ds(0 if side == 0 else 2 * ZONE_DEV, ZONE_DEV)
        return pltpu.make_async_remote_copy(
            src_ref=part.at[rows, :],
            dst_ref=from_next if side == 0 else from_prev,
            send_sem=part_send.at[side],
            recv_sem=part_recv.at[side],
            device_id=device,
            device_id_type=MESH,
        )

    for side in range(2):

        @pl.when(sides[side][0])
        def _(side=side):
            hand_over(side).start()

    grad[...] = part[ZONE_DEV : 2 * ZONE_DEV, :]

    for side, buffer in ((0, from_next), (1, from_prev)):

        @pl.when(sides[1 - side][0])
        def _(side=side, buffer=buffer):
            hand_over(side).wait_recv()
            grad[...] += buffer[...]

    for c in range(n_chunk):
        for q in range(GROUPS):
            own_back(c, q).wait()
            for d in range(1, n_harm):
                back(d, c, q).wait()
        for d in range(1, n_harm):
            arrive(d, c).wait_send()
    for side in range(2):

        @pl.when(sides[side][0])
        def _(side=side):
            hand_over(side).wait_send()
            for c in range(n_chunk):
                for d in range(n_harm):
                    halo(d, c, side).wait_send()


def body(
    n_harm,
    n_node,
    adjoint,
    source,
    rad_coeff,
    capacity,
    inv_diag,
    blocks,
    block_cols,
    zone_of,
    heater_weight,
):
    rows, _, nodes = adjoint.shape
    n_chunk = rows // ROWS
    harmonics = n_harm * rows
    order = np.arange(harmonics).reshape(n_harm, n_chunk, ROWS).transpose(1, 0, 2).reshape(-1)
    basis = fourier_basis(harmonics)
    half = harmonics // 2
    rate_k = np.where(order < half, order, -(order - half)).astype(np.float32)[:, None]
    rate_k = np.broadcast_to(rate_k, (harmonics, WIDTH))

    row_blocks = nodes // 128
    sent = adjoint.reshape(n_chunk, ROWS, n_harm, row_blocks, 128).transpose(2, 0, 3, 1, 4)
    vmem = pl.BlockSpec(memory_space=pltpu.VMEM)
    smem = pl.BlockSpec(memory_space=pltpu.SMEM)
    hbm = pl.BlockSpec(memory_space=pl.ANY)
    piece = (n_harm, n_chunk, ROWS, nodes)
    dma = pltpu.SemaphoreType.DMA
    returned, gradient = pl.pallas_call(
        functools.partial(kernel, n_harm, n_node, n_chunk),
        out_shape=(
            jax.ShapeDtypeStruct(piece, jnp.bfloat16),
            jax.ShapeDtypeStruct((ZONE_DEV, harmonics), jnp.float32),
        ),
        in_specs=[vmem, hbm, hbm, hbm, vmem, vmem, vmem, vmem, smem, vmem, vmem, vmem],
        out_specs=(vmem, vmem),
        scratch_shapes=[pltpu.VMEM((n_harm, 3 * row_blocks, ROWS, 128), jnp.bfloat16)] * n_chunk
        + [
            pltpu.VMEM(piece, jnp.float32),
            pltpu.VMEM(rad_coeff.shape, jnp.bfloat16),
            pltpu.VMEM(blocks.shape, jnp.bfloat16),
            pltpu.VMEM(piece, jnp.bfloat16),
            pltpu.VMEM((256, nodes), jnp.bfloat16),
            pltpu.VMEM((128, harmonics), jnp.float32),
            pltpu.VMEM((ZONE_DEV, harmonics), jnp.float32),
            pltpu.VMEM((ZONE_DEV, harmonics), jnp.float32),
            dma((3 + n_chunk,)),
            dma((n_harm, n_chunk)),
            dma((n_harm, n_chunk)),
            dma((2, n_harm, n_chunk)),
            dma((2, n_harm, n_chunk)),
            dma((n_harm, n_chunk, GROUPS)),
            dma((n_harm, n_chunk, GROUPS)),
            dma((n_chunk, GROUPS)),
            dma((2,)),
            dma((2,)),
        ],
        compiler_params=pltpu.CompilerParams(
            collective_id=0, has_side_effects=True, vmem_limit_bytes=48 * 2**20
        ),
    )(
        sent,
        source.reshape(piece),
        rad_coeff,
        blocks,
        capacity[None, :],
        inv_diag[None, :],
        heater_weight[None, :],
        zone_of[None, :],
        block_cols.T,
        jnp.asarray(basis[:, order]),
        jnp.asarray(basis.T[order]),
        jnp.asarray(rate_k),
    )
    return returned.reshape(n_harm, rows, nodes).transpose(1, 0, 2), gradient


def solution(mesh):
    in_specs = (
        P("harm", None, "node"),
        P(None, ("harm", "node")),
        P(None, ("harm", "node")),
        P(("harm", "node")),
        P(("harm", "node")),
        P(("harm", "node"), None, None, None),
        P(("harm", "node"), None),
        P(("harm", "node")),
        P(("harm", "node")),
    )
    out_specs = (P("harm", None, "node"), P(("harm", "node"), None))
    step = functools.partial(body, mesh.shape["harm"], mesh.shape["node"])
    return jax.shard_map(step, mesh=mesh, in_specs=in_specs, out_specs=out_specs, check_vma=False)
```

profile of v0, /device:TPU:0, one launch (start us, length us, event | category | flops | bytes accessed | tf_op | source)
XLA Modules:
  0.0 73.6 jit_solution(7721104046250517967)
XLA Ops:
  0.6 0.0 copy-start.2
  0.6 0.0 copy-start.3
  0.7 0.0 copy-start.9
  0.7 0.0 copy-start.6
  0.7 0.0 copy-start.7
  0.7 0.0 copy-start.8
  0.7 0.0 copy-start.5
  0.7 0.0 copy-start.4
  0.7 0.0 copy-start.1
  0.7 0.0 copy-start
  0.7 3.1 %reshape.16 = bf16[2,16,4,32,128]{4,3,2,1,0:T(8,128)(2,1)} reshape(bf16[32,4,4096]{2,1,0:T(4,128)(2,1)} %param.12) | data formatting | bytes 2097152 | tf_op jit(solution)/shard_map/reshape | solution.py:347
  3.8 1.9 %copy.22 = bf16[2,16,4,32,128]{4,1,3,0,2:T(8,128)(2,1)S(1)} copy(bf16[2,16,4,32,128]{4,3,2,1,0:T(8,128)(2,1)} %reshape.16) | data formatting | bytes 2097152 | tf_op jit(solution)/shard_map/reshape | solution.py:347
  5.7 0.0 copy-done.9
  5.7 0.1 jit_solution_.3.rate_k
  5.8 0.0 copy-done.2
  5.8 0.0 copy-done.3
  5.8 0.0 copy-done.6
  5.9 0.0 copy-done.7
  5.9 0.0 copy-done.8
  5.9 0.0 copy-done.5
  5.9 0.0 copy-done.4
  5.9 65.3 %shard_map.131 = (bf16[4,2,16,4096]{3,2,1,0:T(8,128)(2,1)S(1)}, f32[40,128]{1,0:T(8,128)S(1)}) custom-call(bf16[4,2,32,16,128]{4,3,2,1,0:T(8,128)(2,1)S(1)} %bitcast.13, f32[4,2,16,4096]{3,2,1,0:T(8,128)S(1)} %bitcast.14, bf16[128,4096]{1,0:T(8,128)(2,1)S(1)} %copy-done.1, bf16[32,4,128,128]{3,2,1,0:T(8,128)(2,1)} %blk_any.1, f32[1,4096]{1,0:T(1,128)S(1)} %bitcast.16, ...), custom_call_target="tpu_custom_call" | custom-call | tf_op jit(solution)/shard_map/pallas_call | solution.py:353
  71.2 1.8 %copy.23 = bf16[4,32,4096]{2,0,1:T(4,128)(2,1)} copy(bf16[4,32,4096]{2,1,0:T(8,128)(2,1)S(1)} %bitcast.15) | data formatting | bytes 2097152 | tf_op jit(solution)/shard_map/reshape | solution.py:399
  73.0 0.6 copy.25
  (2 shorter events, 0.0 us)
Async XLA Ops:
  0.6 5.2 %copy-start.2 = (bf16[128,128]{1,0:T(8,128)(2,1)S(1)}, bf16[128,128]{1,0:T(8,128)(2,1)}, u32[]{:S(2)}) copy-start(bf16[128,128]{1,0:T(8,128)(2,1)} %constant.7.clone.fourier_t) | copy-start | bytes 98308
  0.6 5.2 %copy-start.3 = (bf16[128,128]{1,0:T(8,128)(2,1)S(1)}, bf16[128,128]{1,0:T(8,128)(2,1)}, u32[]{:S(2)}) copy-start(bf16[128,128]{1,0:T(8,128)(2,1)} %constant.6.clone.fourier) | copy-start | bytes 98308
  0.7 5.1 %copy-start.9 = (f32[128]{0:T(128)S(1)}, f32[128]{0:T(128)}, u32[]{:S(2)}) copy-start(f32[128]{0:T(128)} %constant.8.clone) | copy-start | bytes 1540
  0.7 5.2 %copy-start.6 = (f32[4096]{0:T(1024)S(1)}, f32[4096]{0:T(1024)}, u32[]{:S(2)}) copy-start(f32[4096]{0:T(1024)} %param.20) | copy-start | bytes 49156
  0.7 5.2 %copy-start.7 = (s32[4096]{0:T(1024)S(1)}, s32[4096]{0:T(1024)}, u32[]{:S(2)}) copy-start(s32[4096]{0:T(1024)} %param.19) | copy-start | bytes 49156
  0.7 5.2 %copy-start.8 = (s32[32,4]{0,1:T(4,128)S(1)}, s32[32,4]{0,1:T(4,128)}, u32[]{:S(2)}) copy-start(s32[32,4]{0,1:T(4,128)} %param.18) | copy-start | bytes 1540
  0.7 5.2 %copy-start.5 = (f32[4096]{0:T(1024)S(1)}, f32[4096]{0:T(1024)}, u32[]{:S(2)}) copy-start(f32[4096]{0:T(1024)} %param.16) | copy-start | bytes 49156
  0.7 5.2 %copy-start.4 = (f32[4096]{0:T(1024)S(1)}, f32[4096]{0:T(1024)}, u32[]{:S(2)}) copy-start(f32[4096]{0:T(1024)} %param.15) | copy-start | bytes 49156
  0.7 5.2 %copy-start.1 = (bf16[128,4096]{1,0:T(8,128)(2,1)S(1)}, bf16[128,4096]{1,0:T(8,128)(2,1)}, u32[]{:S(2)}) copy-start(bf16[128,4096]{1,0:T(8,128)(2,1)} %rad_any.1) | copy-start | bytes 3145732
  0.7 5.2 %copy-start = (f32[128,4096]{1,0:T(8,128)S(1)}, f32[128,4096]{1,0:T(8,128)}, u32[]{:S(2)}) copy-start(f32[128,4096]{1,0:T(8,128)} %param.13) | copy-start | bytes 6291460
where the time goes:
time: 73.8 us; the launch traced here: 73.6 us
  Pallas kernels  65.3 us (88%)
  local copies, waits for them, and re-layouts  7.5 us (10%)
  between operations  0.81 us (1%)
    pallas_call x1, Pallas kernels, body(): pl.pallas_call(functools.partial(kernel, n_harm, n_node, n_chunk), out_sh...  65.3 us
    reshape x2, local copies, waits for them, and re-layouts, body(): adjoint.reshape(n_chunk, ROWS, n_harm, row_blocks, 128)  4.99 us
    reshape x1, local copies, waits for them, and re-layouts, body(): return (returned.reshape(n_harm, rows, nodes).transpose(1, 0, 2), gradient)  1.78 us

commit v1 on v0

v1 whole, which is shorter than its diff:
```python
import functools
import math

import jax
import jax.numpy as jnp
import numpy as np
from jax import lax
from jax.experimental import pallas as pl
from jax.experimental.pallas import tpu as pltpu
from jax.sharding import PartitionSpec as P

ZONE_DEV = 40
ROWS = 16
PARTS = 4
WIDTH = 256
TILES = 8
MESH = pl.DeviceIdType.MESH
NT = (((1,), (1,)), ((), ()))


def fourier_basis(count):
    sample_index = np.arange(count, dtype=np.float32)[:, None]
    column_index = np.arange(count)[None, :]
    half_count = count // 2
    frequency = np.where(
        column_index <= half_count, column_index, column_index - half_count
    ).astype(np.float32)
    angle = np.float32(2.0 * math.pi) * frequency * sample_index / np.float32(count)
    values_table = np.where(column_index <= half_count, np.cos(angle), np.sin(angle))
    scaling = np.where(
        (column_index == 0) | (column_index == half_count),
        math.sqrt(1.0 / count),
        math.sqrt(2.0 / count),
    ).astype(np.float32)
    return (values_table * scaling).astype(jnp.bfloat16)


def kernel(n_harm, n_node, n_chunk, *refs):
    (
        adj_any,
        src_any,
        rad_any,
        blk_any,
        capacity_any,
        inv_diag_any,
        weight_any,
        zone_any,
        cols_any,
        fourier_any,
        fourier_t_any,
        out,
        grad,
    ) = refs[:13]
    ext = refs[13 : 13 + n_chunk]
    (
        adj,
        src,
        rad,
        blk,
        capacity,
        inv_diag,
        weight,
        zone,
        cols,
        fourier,
        fourier_t,
        stage,
        sent,
        rate_k,
        upd,
        ret,
        select,
        part,
        from_prev,
        from_next,
        load_sem,
        adj_sem,
        own_in,
        in_send,
        in_recv,
        halo_send,
        halo_recv,
        direct_send,
        out_send,
        out_recv,
        own_out,
        part_send,
        part_recv,
    ) = refs[13 + n_chunk :]
    row_blocks = blk.shape[0]
    slots = blk.shape[1]
    nodes = row_blocks * 128
    per_part = row_blocks // PARTS
    chunk_rows = n_harm * ROWS
    me_h = lax.axis_index("harm")
    me_n = lax.axis_index("node")
    pos = me_h * n_node + me_n
    last = n_harm * n_node - 1
    last_n = n_node - 1
    mid = n_harm // 2
    has_prev = pos > 0
    has_next = pos < last
    prev = jnp.maximum(pos - 1, 0)
    following = jnp.minimum(pos + 1, last)
    prev_id = (prev // n_node, prev % n_node)
    next_id = (following // n_node, following % n_node)
    sides = ((has_prev, prev_id, 2), (has_next, next_id, 0))

    low_owner = (me_h == mid - 1) & (me_n == last_n)
    high_owner = (me_h == mid) & (me_n == 0)
    direct = (
        ((me_n == 0) & (me_h < mid), (mid - 1, last_n), mid, 2),
        ((me_n == last_n) & (me_h >= mid), (mid, 0), mid - 1, 0),
    )

    adj_loads = [
        pltpu.make_async_copy(
            adj_any.at[pl.ds(c * ROWS, ROWS)], adj.at[pl.ds(c * ROWS, ROWS)], adj_sem.at[c]
        )
        for c in range(n_chunk)
    ]
    loads = [
        pltpu.make_async_copy(there, here, load_sem.at[i])
        for i, (there, here) in enumerate(
            (
                (weight_any, weight),
                (zone_any, zone),
                (fourier_any, fourier),
                (fourier_t_any, fourier_t),
                (capacity_any, capacity),
                (inv_diag_any, inv_diag),
                (cols_any, cols),
                (rad_any, rad),
                (src_any, src),
                (blk_any, blk),
            )
        )
    ]
    for load in adj_loads:
        load.start()

    barrier = pltpu.get_barrier_semaphore()

    def greet(device):
        pl.semaphore_signal(barrier, inc=1, device_id=device, device_id_type=MESH)

    for d in range(1, n_harm):
        greet((lax.rem(me_h + d, n_harm), me_n))
    for there, device, _ in sides:
        pl.when(there)(functools.partial(greet, device))
    for there, device, _, _ in direct:
        pl.when(there)(functools.partial(greet, device))

    @pl.when(low_owner)
    def _():
        for h in range(mid):
            greet((h, 0))

    @pl.when(high_owner)
    def _():
        for h in range(mid, n_harm):
            greet((h, last_n))

    for load in loads:
        load.start()

    tile_rows = n_harm * ROWS

    def spread(c):
        def step(i, carry):
            at = pl.ds(pl.multiple_of(i * (TILES * 128), TILES * 128), TILES * 128)
            x = adj[c * ROWS : (c + 1) * ROWS, :, at]
            x = x.reshape(tile_rows, TILES * 128).astype(jnp.float32)
            for t in range(TILES):
                stage[t * tile_rows : (t + 1) * tile_rows, :] = x[:, t * 128 : (t + 1) * 128]
            for s in range(n_harm):
                for t in range(TILES):
                    rows = stage[pl.ds(t * tile_rows + s, ROWS, stride=n_harm), :]
                    sent[s, c, i * TILES + t] = rows.astype(jnp.bfloat16)
            return carry

        lax.fori_loop(0, row_blocks // TILES, step, 0)

    def of_part(p, start=0):
        return pl.ds(start + p * per_part, per_part)

    def arrive(d, c, p):
        peer = lax.rem(me_h + d, n_harm)
        return pltpu.make_async_remote_copy(
            src_ref=sent.at[peer, c, of_part(p)],
            dst_ref=ext[c].at[me_h, of_part(p, row_blocks)],
            send_sem=in_send.at[d, c, p],
            recv_sem=in_recv.at[d, c, p],
            device_id=(peer, me_n),
            device_id_type=MESH,
        )

    def own(c):
        return pltpu.make_async_copy(
            sent.at[me_h, c], ext[c].at[me_h, pl.ds(row_blocks, row_blocks)], own_in.at[c]
        )

    def halo(piece, c, p, side, mine=False):
        _, device, place = sides[side]
        if mine:
            source = sent.at[me_h, c, of_part(p)]
        else:
            source = ext[c].at[piece, of_part(p, row_blocks)]
        return pltpu.make_async_remote_copy(
            src_ref=source,
            dst_ref=ext[c].at[piece, of_part(p, place * row_blocks)],
            send_sem=halo_send.at[side, piece, c, p],
            recv_sem=halo_recv.at[side, piece, c, p],
            device_id=device,
            device_id_type=MESH,
        )

    def direct_halo(c, p, side):
        _, device, s, place = direct[side]
        return pltpu.make_async_remote_copy(
            src_ref=sent.at[s, c, of_part(p)],
            dst_ref=ext[c].at[me_h, of_part(p, place * row_blocks)],
            send_sem=direct_send.at[c, p],
            recv_sem=halo_recv.at[side, me_h, c, p],
            device_id=device,
            device_id_type=MESH,
        )

    def piece_of(d):
        return lax.rem(me_h - d + n_harm, n_harm)

    def forwards(d, side):
        piece = piece_of(d)
        if side == 0:
            return has_prev & jnp.logical_not(high_owner & (piece < mid))
        return has_next & jnp.logical_not(low_owner & (piece >= mid))

    def start_halo(d, c, p):
        for side in range(2):

            @pl.when(forwards(d, side))
            def _(side=side):
                halo(piece_of(d), c, p, side, mine=d == 0).start()

    order = sorted(range(1, n_harm), key=lambda d: abs(d - mid))

    def send(c):
        for p in range(PARTS):
            for d in order:
                arrive(d, c, p).start()
            start_halo(0, c, p)
            for side in range(2):

                @pl.when(direct[side][0])
                def _(side=side, p=p):
                    direct_halo(c, p, side).start()

        own(c).start()

    adj_loads[0].wait()
    spread(0)
    one = jnp.int32(1)
    zero = jnp.int32(0)
    expected = (
        jnp.int32(n_harm - 1)
        + jnp.where(has_prev, one, zero)
        + jnp.where(has_next, one, zero)
        + jnp.where(direct[0][0], one, zero)
        + jnp.where(direct[1][0], one, zero)
        + jnp.where(low_owner, jnp.int32(mid), zero)
        + jnp.where(high_owner, jnp.int32(n_harm - mid), zero)
    )
    pl.semaphore_wait(barrier, expected)
    send(0)
    for c in range(1, n_chunk):
        adj_loads[c].wait()
        spread(c)
        send(c)

    half = chunk_rows // 2
    for c in range(n_chunk):
        row = lax.broadcasted_iota(jnp.int32, (chunk_rows, 128), 0)
        k = (row // ROWS) * (n_chunk * ROWS) + c * ROWS + row % ROWS
        half_k = n_harm * n_chunk * ROWS // 2
        rate = jnp.where(k < half_k, k, half_k - k).astype(jnp.float32)
        rate_k[c * chunk_rows : (c + 1) * chunk_rows, :] = rate

    for load in loads:
        load.wait()

    zone_row = lax.broadcasted_iota(jnp.int32, (128, WIDTH), 0)

    def select_step(i, carry):
        at = pl.ds(pl.multiple_of(i * WIDTH, WIDTH), WIDTH)
        hit = zone_row == (zone[:, at] - (pos - 1) * ZONE_DEV)
        w = weight[:, at]
        high = w.astype(jnp.bfloat16).astype(jnp.float32)
        select[0:128, at] = jnp.where(hit, high, 0.0).astype(jnp.bfloat16)
        select[128:256, at] = jnp.where(hit, w - high, 0.0).astype(jnp.bfloat16)
        return carry

    lax.fori_loop(0, nodes // WIDTH, select_step, 0)

    def block_of(c, index):
        return jnp.concatenate([ext[c][h, index] for h in range(n_harm)], axis=0)

    def local_part(p):
        def local_step(i, carry):
            at = pl.ds(pl.multiple_of(i * WIDTH, WIDTH), WIDTH)
            first = row_blocks + i * (WIDTH // 128)
            pieces = [
                jnp.concatenate([block_of(c, first + t) for t in range(WIDTH // 128)], axis=1)
                for c in range(n_chunk)
            ]
            field = jnp.concatenate(pieces, axis=0) if n_chunk > 1 else pieces[0]
            samples = jnp.dot(fourier[...], field, preferred_element_type=jnp.float32)
            weighted = (rad[:, at].astype(jnp.float32) * samples).astype(jnp.bfloat16)
            radiative = jnp.dot(fourier_t[...], weighted, preferred_element_type=jnp.float32)
            cap = capacity[:, at]
            for c in range(n_chunk):
                lam = pieces[c].astype(jnp.float32)
                swapped = jnp.concatenate([lam[half:], lam[:half]], axis=0)
                rows = slice(c * chunk_rows, (c + 1) * chunk_rows)
                k = jnp.concatenate([rate_k[rows, :]] * (WIDTH // 128), axis=1)
                rate = k * swapped
                rest = src[:, c, :, at].reshape(chunk_rows, WIDTH) - (cap * rate + radiative[rows])
                src[:, c, :, at] = rest.reshape(n_harm, ROWS, WIDTH)
            return carry

        steps = nodes // PARTS // WIDTH
        lax.fori_loop(p * steps, (p + 1) * steps, local_step, 0)

    def back(d, c, p):
        peer = lax.rem(me_h + d, n_harm)
        return pltpu.make_async_remote_copy(
            src_ref=upd.at[peer, c, of_part(p)],
            dst_ref=ret.at[me_h, c, of_part(p)],
            send_sem=out_send.at[d, c, p],
            recv_sem=out_recv.at[d, c, p],
            device_id=(peer, me_n),
            device_id_type=MESH,
        )

    def own_back(c, p):
        return pltpu.make_async_copy(
            upd.at[me_h, c, of_part(p)], ret.at[me_h, c, of_part(p)], own_out.at[c, p]
        )

    def conduct(c, p):
        def block_step(i, carry):
            b = p * per_part + i
            at = pl.ds(pl.multiple_of(b * 128, 128), 128)
            lam = block_of(c, row_blocks + b)
            taken = [lam]
            for s in range(1, slots):
                col = cols[s, b] - (pos - 1) * row_blocks
                col = jnp.minimum(jnp.maximum(col, 0), 3 * row_blocks - 1)
                taken.append(block_of(c, col))
            conductance = jnp.concatenate([blk[b, s] for s in range(slots)], axis=1)
            conduction = lax.dot_general(
                jnp.concatenate(taken, axis=1),
                conductance,
                NT,
                preferred_element_type=jnp.float32,
            )
            residual = src[:, c, :, at].reshape(chunk_rows, 128) - conduction
            new = lam.astype(jnp.float32) + inv_diag[:, at] * residual
            upd[:, c, b] = new.astype(jnp.bfloat16).reshape(n_harm, ROWS, 128)
            return carry

        lax.fori_loop(0, per_part, block_step, 0, unroll=2)
        for d in order:
            back(d, c, p).start()
        own_back(c, p).start()

    def wait_halo(c):
        for side in range(2):

            @pl.when(sides[1 - side][0])
            def _(side=side):
                for p in range(PARTS):
                    for piece in range(n_harm):
                        halo(piece, c, p, side).wait_recv()

    for c in range(n_chunk):
        own(c).wait()
        for p in range(PARTS):
            for d in range(1, n_harm):
                arrive(d, c, p).wait_recv()
                start_halo(d, c, p)
            if c == n_chunk - 1:
                local_part(p)

    for c in range(n_chunk):
        wait_halo(c)
        for p in range(PARTS):
            conduct(c, p)

    part[...] = jnp.zeros_like(part)
    wide = 512 // 128

    def gradient_step(i, carry):
        at = pl.ds(pl.multiple_of(i * 512, 512), 512)
        new = jnp.concatenate(
            [
                upd[:, :, i * wide + t].reshape(n_harm * n_chunk * ROWS, 128)
                for t in range(wide)
            ],
            axis=1,
        )
        both = lax.dot_general(select[:, at], new, NT, preferred_element_type=jnp.float32)
        part[...] += both[0:128] + both[128:256]
        return carry

    lax.fori_loop(0, nodes // 512, gradient_step, 0)

    def hand_over(side):
        _, device, place = sides[side]
        rows = pl.ds(0 if side == 0 else 2 * ZONE_DEV, ZONE_DEV)
        return pltpu.make_async_remote_copy(
            src_ref=part.at[rows, :],
            dst_ref=from_next if side == 0 else from_prev,
            send_sem=part_send.at[side],
            recv_sem=part_recv.at[side],
            device_id=device,
            device_id_type=MESH,
        )

    for side in range(2):

        @pl.when(sides[side][0])
        def _(side=side):
            hand_over(side).start()

    grad[...] = part[ZONE_DEV : 2 * ZONE_DEV, :]

    for side, buffer in ((0, from_next), (1, from_prev)):

        @pl.when(sides[1 - side][0])
        def _(side=side, buffer=buffer):
            hand_over(side).wait_recv()
            grad[...] += buffer[...]

    def gather(c, p):
        def step(i, carry):
            b = p * per_part + i * TILES
            at = pl.ds(pl.multiple_of(b * 128, 128), TILES * 128)
            for s in range(n_harm):
                for t in range(TILES):
                    stage[pl.ds(t * tile_rows + s, ROWS, stride=n_harm), :] = ret[
                        s, c, b + t
                    ].astype(jnp.float32)
            x = jnp.concatenate(
                [stage[t * tile_rows : (t + 1) * tile_rows, :] for t in range(TILES)], axis=1
            )
            x = x.astype(jnp.bfloat16).reshape(ROWS, n_harm, TILES * 128)
            out[c * ROWS : (c + 1) * ROWS, :, at] = x
            return carry

        lax.fori_loop(0, per_part // TILES, step, 0)

    for c in range(n_chunk):
        for p in range(PARTS):
            own_back(c, p).wait()
            for d in range(1, n_harm):
                back(d, c, p).wait_recv()
            gather(c, p)

    for c in range(n_chunk):
        for p in range(PARTS):
            for d in range(1, n_harm):
                arrive(d, c, p).wait_send()
                back(d, c, p).wait_send()
            for side in range(2):

                @pl.when(direct[side][0])
                def _(side=side, c=c, p=p):
                    direct_halo(c, p, side).wait_send()

                for d in range(n_harm):

                    @pl.when(forwards(d, side))
                    def _(side=side, d=d, c=c, p=p):
                        halo(piece_of(d), c, p, side, mine=d == 0).wait_send()

    for side in range(2):

        @pl.when(sides[side][0])
        def _(side=side):
            hand_over(side).wait_send()


def body(
    n_harm,
    n_node,
    adjoint,
    source,
    rad_coeff,
    capacity,
    inv_diag,
    blocks,
    block_cols,
    zone_of,
    heater_weight,
):
    rows, _, nodes = adjoint.shape
    n_chunk = rows // ROWS
    harmonics = n_harm * rows
    order = np.arange(harmonics).reshape(n_harm, n_chunk, ROWS).transpose(1, 0, 2).reshape(-1)
    basis = fourier_basis(harmonics)

    row_blocks = nodes // 128
    vmem = pl.BlockSpec(memory_space=pltpu.VMEM)
    hbm = pl.BlockSpec(memory_space=pltpu.HBM)
    piece = (n_harm, n_chunk, ROWS, nodes)
    tiles = (n_harm, n_chunk, row_blocks, ROWS, 128)
    line = (1, nodes)
    dma = pltpu.SemaphoreType.DMA
    updated, gradient = pl.pallas_call(
        functools.partial(kernel, n_harm, n_node, n_chunk),
        out_shape=(
            jax.ShapeDtypeStruct(adjoint.shape, jnp.bfloat16),
            jax.ShapeDtypeStruct((ZONE_DEV, harmonics), jnp.float32),
        ),
        in_specs=[hbm] * 11,
        out_specs=(vmem, vmem),
        scratch_shapes=[pltpu.VMEM((n_harm, 3 * row_blocks, ROWS, 128), jnp.bfloat16)] * n_chunk
        + [
            pltpu.VMEM(adjoint.shape, jnp.bfloat16),
            pltpu.VMEM(piece, jnp.float32),
            pltpu.VMEM(rad_coeff.shape, jnp.bfloat16),
            pltpu.VMEM(blocks.shape, jnp.bfloat16),
            pltpu.VMEM(line, jnp.float32),
            pltpu.VMEM(line, jnp.float32),
            pltpu.VMEM(line, jnp.float32),
            pltpu.VMEM(line, jnp.int32),
            pltpu.SMEM(block_cols.shape[::-1], jnp.int32),
            pltpu.VMEM((harmonics, harmonics), jnp.bfloat16),
            pltpu.VMEM((harmonics, harmonics), jnp.bfloat16),
            pltpu.VMEM((TILES * n_harm * ROWS, 128), jnp.float32),
            pltpu.VMEM(tiles, jnp.bfloat16),
            pltpu.VMEM((harmonics, 128), jnp.float32),
            pltpu.VMEM(tiles, jnp.bfloat16),
            pltpu.VMEM(tiles, jnp.bfloat16),
            pltpu.VMEM((256, nodes), jnp.bfloat16),
            pltpu.VMEM((128, harmonics), jnp.float32),
            pltpu.VMEM((ZONE_DEV, harmonics), jnp.float32),
            pltpu.VMEM((ZONE_DEV, harmonics), jnp.float32),
            dma((10,)),
            dma((n_chunk,)),
            dma((n_chunk,)),
            dma((n_harm, n_chunk, PARTS)),
            dma((n_harm, n_chunk, PARTS)),
            dma((2, n_harm, n_chunk, PARTS)),
            dma((2, n_harm, n_chunk, PARTS)),
            dma((n_chunk, PARTS)),
            dma((n_harm, n_chunk, PARTS)),
            dma((n_harm, n_chunk, PARTS)),
            dma((n_chunk, PARTS)),
            dma((2,)),
            dma((2,)),
        ],
        compiler_params=pltpu.CompilerParams(
            collective_id=0, has_side_effects=True, vmem_limit_bytes=48 * 2**20
        ),
    )(
        *(
            pltpu.with_memory_space_constraint(x, pltpu.HBM)
            for x in (
                adjoint,
                source.reshape(piece),
                rad_coeff,
                blocks,
                capacity[None, :],
                inv_diag[None, :],
                heater_weight[None, :],
                zone_of[None, :],
                block_cols.T,
                jnp.asarray(basis[:, order]),
                jnp.asarray(basis.T[order]),
            )
        )
    )
    return updated, gradient


def solution(mesh):
    in_specs = (
        P("harm", None, "node"),
        P(None, ("harm", "node")),
        P(None, ("harm", "node")),
        P(("harm", "node")),
        P(("harm", "node")),
        P(("harm", "node"), None, None, None),
        P(("harm", "node"), None),
        P(("harm", "node")),
        P(("harm", "node")),
    )
    out_specs = (P("harm", None, "node"), P(("harm", "node"), None))
    step = functools.partial(body, mesh.shape["harm"], mesh.shape["node"])
    return jax.shard_map(step, mesh=mesh, in_specs=in_specs, out_specs=out_specs, check_vma=False)
```

time: 73.8 us -> 61.9 us (0.84)
  local copies, waits for them, and re-layouts: 7.5 us -> 1.58 us
  Pallas kernels: 65.3 us -> 59.5 us
    reshape x3 -> x0, local copies, waits for them, and re-layouts: 6.77 us -> none  [the longest x2 4.99 us: body(): adjoint.reshape(n_chunk, ROWS, n_harm, row_blocks, 128)]
    pallas_call x1, Pallas kernels: 65.3 us -> 59.5 us  [body(): pl.pallas_call(functools.partial(kernel, n_harm, n_node, n_chunk), out_sh...]
    unnamed x21 -> x2, local copies, waits for them, and re-layouts: 0.66 us -> 1.58 us
where the time goes in v1:
time: 61.9 us; the launch traced here: 61.8 us
  Pallas kernels  59.5 us (96%)
  local copies, waits for them, and re-layouts  1.58 us (3%)
  between operations  0.64 us (1%)
    pallas_call x1, Pallas kernels, body(): pl.pallas_call(functools.partial(kernel, n_harm, n_node, n_chunk), out_sh...  59.5 us
    unnamed x2, local copies, waits for them, and re-layouts  1.58 us

profile of v1, /device:TPU:0, one launch (start us, length us, event | category | flops | bytes accessed | tf_op | source)
XLA Modules:
  0.0 61.8 jit_solution(5013662180988958889)
XLA Ops:
  0.6 59.5 %shard_map.122 = (bf16[32,4,4096]{2,1,0:T(4,128)(2,1)S(1)}, f32[40,128]{1,0:T(8,128)S(1)}) custom-call(bf16[32,4,4096]{2,1,0:T(4,128)(2,1)} %refs_0_.1, f32[4,2,16,4096]{3,2,1,0:T(8,128)} %bitcast.6, bf16[128,4096]{1,0:T(8,128)(2,1)} %refs_2_.1, bf16[32,4,128,128]{3,2,1,0:T(8,128)(2,1)} %refs_3_.1, f32[1,4096]{1,0:T(1,128)} %bitcast.7, f32[1,4096]{1,0:T(1,128)} %bitcast.8, ...), custom_call_target="tpu_custom_call" | custom-call | tf_op jit(solution)/shard_map/pallas_call | solution.py:519
  60.2 1.0 %copy.15 = bf16[32,4,4096]{2,1,0:T(4,128)(2,1)} copy(bf16[32,4,4096]{2,1,0:T(4,128)(2,1)S(1)} %get-tuple-element.4) | data formatting | bytes 2097152
  61.2 0.6 copy.16

commit v2 on v1

--- a/solution.py
+++ b/solution.py
@@ -12,6 +12,8 @@
 ZONE_DEV = 40
 ROWS = 16
 PARTS = 4
+EARLY = 0
+LAG = 0
 WIDTH = 256
 TILES = 8
 MESH = pl.DeviceIdType.MESH
@@ -86,6 +88,10 @@
         own_out,
         part_send,
         part_recv,
+        held,
+        depart_send,
+        bend_send,
+        bend_recv,
     ) = refs[13 + n_chunk :]
     row_blocks = blk.shape[0]
     slots = blk.shape[1]
@@ -106,12 +112,52 @@
     next_id = (following // n_node, following % n_node)
     sides = ((has_prev, prev_id, 2), (has_next, next_id, 0))
 
-    low_owner = (me_h == mid - 1) & (me_n == last_n)
-    high_owner = (me_h == mid) & (me_n == 0)
-    direct = (
-        ((me_n == 0) & (me_h < mid), (mid - 1, last_n), mid, 2),
-        ((me_n == last_n) & (me_h >= mid), (mid, 0), mid - 1, 0),
-    )
+    at_first = me_n == 0
+    at_last = me_n == last_n
+
+    def straight(h, other):
+        return jnp.equal(jnp.greater_equal(h, mid), jnp.greater_equal(other, mid))
+
+    direct = [
+        [
+            (at_first & straight(me_h, t - 1), (t - 1, last_n), t, 2),
+            (at_last & straight(me_h, t), (t, 0), t - 1, 0),
+        ]
+        for t in range(1, n_harm)
+    ]
+    greeted = [(there, device) for there, device, _ in sides]
+    greeted += [(there, device) for pair in direct for there, device, _, _ in pair]
+    for h in range(n_harm):
+        greeted.append((at_first & (me_h > 0) & straight(h, me_h), (h, last_n)))
+        greeted.append((at_last & (me_h < n_harm - 1) & straight(h, me_h), (h, 0)))
+
+    low = me_h < mid
+    high = me_h >= mid
+    origin = (at_first & high, at_last & low)
+    goal = ((mid - 1, last_n), (mid, 0))
+    at_goal = ((me_h == mid - 1) & at_last, (me_h == mid) & at_first)
+    group = (mid, mid - 1)
+    far = (range(mid, n_harm), range(mid))
+    start_n = (0, last_n)
+
+    def way_n(p, side):
+        step = 2 * (p % (n_node // 2))
+        return last_n - step if side else step
+
+    def at_way(p, side):
+        return (low if side else high) & (me_n == way_n(p, side))
+
+    bends = [
+        (p, side) for p in range(PARTS) for side in range(2) if way_n(p, side) != start_n[side]
+    ]
+    for side in range(2):
+        for n in sorted({way_n(p, side) for p in range(PARTS)}):
+            greeted += [(at_goal[side], (h, n)) for h in far[side]]
+            here = (low if side else high) & (me_n == n)
+            greeted.append((here, goal[side]))
+            if n != start_n[side]:
+                greeted.append((here, (me_h, start_n[side])))
+                greeted.append((origin[side], (me_h, n)))
 
     adj_loads = [
         pltpu.make_async_copy(
@@ -146,20 +192,8 @@
 
     for d in range(1, n_harm):
         greet((lax.rem(me_h + d, n_harm), me_n))
-    for there, device, _ in sides:
+    for there, device in greeted:
         pl.when(there)(functools.partial(greet, device))
-    for there, device, _, _ in direct:
-        pl.when(there)(functools.partial(greet, device))
-
-    @pl.when(low_owner)
-    def _():
-        for h in range(mid):
-            greet((h, 0))
-
-    @pl.when(high_owner)
-    def _():
-        for h in range(mid, n_harm):
-            greet((h, last_n))
 
     for load in loads:
         load.start()
@@ -215,25 +249,61 @@
             device_id_type=MESH,
         )
 
-    def direct_halo(c, p, side):
-        _, device, s, place = direct[side]
+    def direct_halo(c, p, t, side):
+        _, device, s, place = direct[t][side]
         return pltpu.make_async_remote_copy(
             src_ref=sent.at[s, c, of_part(p)],
             dst_ref=ext[c].at[me_h, of_part(p, place * row_blocks)],
-            send_sem=direct_send.at[c, p],
+            send_sem=direct_send.at[t, c, p],
             recv_sem=halo_recv.at[side, me_h, c, p],
             device_id=device,
             device_id_type=MESH,
         )
 
+    def depart(c, p, side):
+        bent = (p, side) in bends
+        if bent:
+            landing, done = held.at[p, c], bend_recv.at[p, c]
+        else:
+            landing = ext[c].at[me_h, of_part(p, sides[side][2] * row_blocks)]
+            done = halo_recv.at[side, me_h, c, p]
+        return pltpu.make_async_remote_copy(
+            src_ref=sent.at[group[side], c, of_part(p)],
+            dst_ref=landing,
+            send_sem=depart_send.at[c, p],
+            recv_sem=done,
+            device_id=(me_h, way_n(p, side)) if bent else goal[side],
+            device_id_type=MESH,
+        )
+
+    def relay_on(c, p, side):
+        return pltpu.make_async_remote_copy(
+            src_ref=held.at[p, c],
+            dst_ref=ext[c].at[me_h, of_part(p, sides[side][2] * row_blocks)],
+            send_sem=bend_send.at[p, c],
+            recv_sem=halo_recv.at[side, me_h, c, p],
+            device_id=goal[side],
+            device_id_type=MESH,
+        )
+
+    def relay(c):
+        for p, side in bends:
+
+            @pl.when(at_way(p, side))
+            def _(p=p, side=side):
+                depart(c, p, side).wait_recv()
+                relay_on(c, p, side).start()
+
     def piece_of(d):
         return lax.rem(me_h - d + n_harm, n_harm)
 
     def forwards(d, side):
         piece = piece_of(d)
         if side == 0:
-            return has_prev & jnp.logical_not(high_owner & (piece < mid))
-        return has_next & jnp.logical_not(low_owner & (piece >= mid))
+            skip = straight(piece, me_h - 1) | (me_h == mid)
+            return has_prev & jnp.logical_not(at_first & skip)
+        skip = straight(piece, me_h + 1) | (me_h + 1 == mid)
+        return has_next & jnp.logical_not(at_last & skip)
 
     def start_halo(d, c, p):
         for side in range(2):
@@ -245,36 +315,37 @@
     order = sorted(range(1, n_harm), key=lambda d: abs(d - mid))
 
     def send(c):
+        for side in range(2):
+
+            @pl.when(origin[side])
+            def _(side=side):
+                for p in range(PARTS):
+                    depart(c, p, side).start()
+
         for p in range(PARTS):
             for d in order:
                 arrive(d, c, p).start()
             start_halo(0, c, p)
-            for side in range(2):
-
-                @pl.when(direct[side][0])
-                def _(side=side, p=p):
-                    direct_halo(c, p, side).start()
+            for t in range(n_harm - 1):
+                for side in range(2):
+
+                    @pl.when(direct[t][side][0])
+                    def _(t=t, side=side, p=p):
+                        direct_halo(c, p, t, side).start()
 
         own(c).start()
 
     adj_loads[0].wait()
     spread(0)
-    one = jnp.int32(1)
-    zero = jnp.int32(0)
-    expected = (
-        jnp.int32(n_harm - 1)
-        + jnp.where(has_prev, one, zero)
-        + jnp.where(has_next, one, zero)
-        + jnp.where(direct[0][0], one, zero)
-        + jnp.where(direct[1][0], one, zero)
-        + jnp.where(low_owner, jnp.int32(mid), zero)
-        + jnp.where(high_owner, jnp.int32(n_harm - mid), zero)
-    )
+    expected = jnp.int32(n_harm - 1)
+    for there, _ in greeted:
+        expected = expected + jnp.where(there, jnp.int32(1), jnp.int32(0))
     pl.semaphore_wait(barrier, expected)
     send(0)
     for c in range(1, n_chunk):
         adj_loads[c].wait()
         spread(c)
+        relay(c - 1)
         send(c)
 
     half = chunk_rows // 2
@@ -300,6 +371,7 @@
         return carry
 
     lax.fori_loop(0, nodes // WIDTH, select_step, 0)
+    relay(n_chunk - 1)
 
     def block_of(c, index):
         return jnp.concatenate([ext[c][h, index] for h in range(n_harm)], axis=0)
@@ -382,18 +454,31 @@
                     for piece in range(n_harm):
                         halo(piece, c, p, side).wait_recv()
 
+    def take(c, p):
+        if p == 0:
+            own(c).wait()
+        for d in range(1, n_harm):
+            arrive(d, c, p).wait_recv()
+            start_halo(d, c, p)
+
+    final = n_chunk - 1
+    for c in range(final):
+        for p in range(PARTS):
+            take(c, p)
+    done = 0
+    for p in range(PARTS):
+        take(final, p)
+        local_part(p)
+        if final > 0 and p >= EARLY:
+            if done == 0:
+                wait_halo(0)
+            while done < p - LAG + 1:
+                conduct(0, done)
+                done += 1
     for c in range(n_chunk):
-        own(c).wait()
-        for p in range(PARTS):
-            for d in range(1, n_harm):
-                arrive(d, c, p).wait_recv()
-                start_halo(d, c, p)
-            if c == n_chunk - 1:
-                local_part(p)
-
-    for c in range(n_chunk):
-        wait_halo(c)
-        for p in range(PARTS):
+        if c > 0 or done == 0:
+            wait_halo(c)
+        for p in range(done if c == 0 else 0, PARTS):
             conduct(c, p)
 
     part[...] = jnp.zeros_like(part)
@@ -472,16 +557,31 @@
                 arrive(d, c, p).wait_send()
                 back(d, c, p).wait_send()
             for side in range(2):
-
-                @pl.when(direct[side][0])
-                def _(side=side, c=c, p=p):
-                    direct_halo(c, p, side).wait_send()
+                for t in range(n_harm - 1):
+
+                    @pl.when(direct[t][side][0])
+                    def _(t=t, side=side, c=c, p=p):
+                        direct_halo(c, p, t, side).wait_send()
 
                 for d in range(n_harm):
 
                     @pl.when(forwards(d, side))
                     def _(side=side, d=d, c=c, p=p):
                         halo(piece_of(d), c, p, side, mine=d == 0).wait_send()
+
+    for c in range(n_chunk):
+        for side in range(2):
+
+            @pl.when(origin[side])
+            def _(c=c, side=side):
+                for p in range(PARTS):
+                    depart(c, p, side).wait_send()
+
+        for p, side in bends:
+
+            @pl.when(at_way(p, side))
+            def _(c=c, p=p, side=side):
+                relay_on(c, p, side).wait_send()
 
     for side in range(2):
 
@@ -553,12 +653,16 @@
             dma((n_harm, n_chunk, PARTS)),
             dma((2, n_harm, n_chunk, PARTS)),
             dma((2, n_harm, n_chunk, PARTS)),
-            dma((n_chunk, PARTS)),
+            dma((n_harm - 1, n_chunk, PARTS)),
             dma((n_harm, n_chunk, PARTS)),
             dma((n_harm, n_chunk, PARTS)),
             dma((n_chunk, PARTS)),
             dma((2,)),
             dma((2,)),
+            pltpu.VMEM((PARTS, n_chunk, row_blocks // PARTS, ROWS, 128), jnp.bfloat16),
+            dma((n_chunk, PARTS)),
+            dma((PARTS, n_chunk)),
+            dma((PARTS, n_chunk)),
         ],
         compiler_params=pltpu.CompilerParams(
             collective_id=0, has_side_effects=True, vmem_limit_bytes=48 * 2**20

time: 61.9 us -> 58.7 us (0.948); the launches traced: 61.8 us -> 57.7 us
  Pallas kernels: 59.5 us -> 55.5 us
    pallas_call x1, Pallas kernels: 59.5 us -> 55.5 us  [body(): pl.pallas_call(functools.partial(kernel, n_harm, n_node, n_chunk), out_sh...]
where the time goes in v2:
time: 58.7 us; the launch traced here: 57.7 us
  Pallas kernels  55.5 us (95%)
  local copies, waits for them, and re-layouts  1.58 us (3%)
  between operations  0.64 us (1%)
    pallas_call x1, Pallas kernels, body(): pl.pallas_call(functools.partial(kernel, n_harm, n_node, n_chunk), out_sh...  55.5 us
    unnamed x2, local copies, waits for them, and re-layouts  1.58 us

profile of v2, /device:TPU:0, one launch (start us, length us, event | category | flops | bytes accessed | tf_op | source)
XLA Modules:
  0.0 57.7 jit_solution(10997429401913199304)
XLA Ops:
  0.6 55.5 %shard_map.122 = (bf16[32,4,4096]{2,1,0:T(4,128)(2,1)S(1)}, f32[40,128]{1,0:T(8,128)S(1)}) custom-call(bf16[32,4,4096]{2,1,0:T(4,128)(2,1)} %refs_0_.1, f32[4,2,16,4096]{3,2,1,0:T(8,128)} %bitcast.6, bf16[128,4096]{1,0:T(8,128)(2,1)} %refs_2_.1, bf16[32,4,128,128]{3,2,1,0:T(8,128)(2,1)} %refs_3_.1, f32[1,4096]{1,0:T(1,128)} %bitcast.7, f32[1,4096]{1,0:T(1,128)} %bitcast.8, ...), custom_call_target="tpu_custom_call" | custom-call | tf_op jit(solution)/shard_map/pallas_call | solution.py:619
  56.1 1.0 %copy.15 = bf16[32,4,4096]{2,1,0:T(4,128)(2,1)} copy(bf16[32,4,4096]{2,1,0:T(4,128)(2,1)S(1)} %get-tuple-element.4) | data formatting | bytes 2097152
  57.1 0.6 %copy.16 = f32[40,128]{1,0:T(8,128)} copy(f32[40,128]{1,0:T(8,128)S(1)} %get-tuple-element.5) | data formatting | bytes 40960

commit v3 on v2

--- a/solution.py
+++ b/solution.py
@@ -12,6 +12,10 @@
 ZONE_DEV = 40
 ROWS = 16
 PARTS = 4
+MAJOR = ()
+ORDER = [3, 2, 1]
+BACK = [2, 1, 3]
+SLICES = 4
 EARLY = 0
 LAG = 0
 WIDTH = 256
@@ -140,24 +144,21 @@
     far = (range(mid, n_harm), range(mid))
     start_n = (0, last_n)
 
-    def way_n(p, side):
-        step = 2 * (p % (n_node // 2))
-        return last_n - step if side else step
+    def way_n(p, side, h):
+        column = p % 4 if p % 4 < 3 else 1 + h % 2
+        return last_n - 2 * column - (1 - side)
 
     def at_way(p, side):
-        return (low if side else high) & (me_n == way_n(p, side))
-
-    bends = [
-        (p, side) for p in range(PARTS) for side in range(2) if way_n(p, side) != start_n[side]
-    ]
-    for side in range(2):
-        for n in sorted({way_n(p, side) for p in range(PARTS)}):
-            greeted += [(at_goal[side], (h, n)) for h in far[side]]
-            here = (low if side else high) & (me_n == n)
-            greeted.append((here, goal[side]))
-            if n != start_n[side]:
-                greeted.append((here, (me_h, start_n[side])))
-                greeted.append((origin[side], (me_h, n)))
+        return (low if side else high) & (me_n == way_n(p, side, me_h))
+
+    bends = [(p, side) for p in range(PARTS) for side in range(2) if side == 0 or p % 4]
+    for p in range(PARTS):
+        for side in range(2):
+            greeted += [(at_goal[side], (h, way_n(p, side, h))) for h in far[side]]
+            greeted.append((at_way(p, side), goal[side]))
+            if (p, side) in bends:
+                greeted.append((at_way(p, side), (me_h, start_n[side])))
+                greeted.append((origin[side], (me_h, way_n(p, side, me_h))))
 
     adj_loads = [
         pltpu.make_async_copy(
@@ -272,7 +273,7 @@
             dst_ref=landing,
             send_sem=depart_send.at[c, p],
             recv_sem=done,
-            device_id=(me_h, way_n(p, side)) if bent else goal[side],
+            device_id=(me_h, way_n(p, side, me_h)) if bent else goal[side],
             device_id_type=MESH,
         )
 
@@ -312,7 +313,8 @@
             def _(side=side):
                 halo(piece_of(d), c, p, side, mine=d == 0).start()
 
-    order = sorted(range(1, n_harm), key=lambda d: abs(d - mid))
+    order = ORDER if n_harm == 4 else list(range(1, n_harm))
+    back_order = BACK if n_harm == 4 else list(range(1, n_harm))
 
     def send(c):
         for side in range(2):
@@ -322,9 +324,14 @@
                 for p in range(PARTS):
                     depart(c, p, side).start()
 
+        if c in MAJOR:
+            for d in order:
+                for p in range(PARTS):
+                    arrive(d, c, p).start()
         for p in range(PARTS):
-            for d in order:
-                arrive(d, c, p).start()
+            if c not in MAJOR:
+                for d in order:
+                    arrive(d, c, p).start()
             start_halo(0, c, p)
             for t in range(n_harm - 1):
                 for side in range(2):
@@ -441,7 +448,7 @@
             return carry
 
         lax.fori_loop(0, per_part, block_step, 0, unroll=2)
-        for d in order:
+        for d in back_order:
             back(d, c, p).start()
         own_back(c, p).start()
 
@@ -588,6 +595,18 @@
         @pl.when(sides[side][0])
         def _(side=side):
             hand_over(side).wait_send()
+
+
+def write_out(updated, gradient, out, grad, sems):
+    rows = updated.shape[0] // SLICES
+    copies = [pltpu.make_async_copy(gradient, grad, sems.at[SLICES])]
+    for i in range(SLICES):
+        at = pl.ds(i * rows, rows)
+        copies.append(pltpu.make_async_copy(updated.at[at], out.at[at], sems.at[i]))
+    for copy in copies:
+        copy.start()
+    for copy in copies:
+        copy.wait()
 
 
 def body(
@@ -685,7 +704,19 @@
             )
         )
     )
-    return updated, gradient
+    return pl.pallas_call(
+        write_out,
+        out_shape=(
+            jax.ShapeDtypeStruct(updated.shape, updated.dtype),
+            jax.ShapeDtypeStruct(gradient.shape, gradient.dtype),
+        ),
+        in_specs=[vmem, vmem],
+        out_specs=(hbm, hbm),
+        scratch_shapes=[dma((SLICES + 1,))],
+    )(
+        pltpu.with_memory_space_constraint(updated, pltpu.VMEM),
+        pltpu.with_memory_space_constraint(gradient, pltpu.VMEM),
+    )
 
 
 def solution(mesh):

time: 58.7 us -> 58.1 us (0.990)
  the two profiles are of different devices: /device:TPU:0 before, /device:TPU:16 now
where the time goes in v3:
time: 58.1 us; the launch traced here: 58 us
  Pallas kernels  57.4 us (99%)
  between operations  0.64 us (1%)
    pallas_call x1, Pallas kernels, body(): pl.pallas_call(functools.partial(kernel, n_harm, n_node, n_chunk), out_sh...  56.3 us

profile of v3, /device:TPU:16, one launch (start us, length us, event | category | flops | bytes accessed | tf_op | source)
XLA Modules:
  0.0 58.0 jit_solution(3570911422819493710)
XLA Ops:
  0.6 56.3 %shard_map.122 = (bf16[32,4,4096]{2,1,0:T(4,128)(2,1)S(1)}, f32[40,128]{1,0:T(8,128)S(1)}) custom-call(bf16[32,4,4096]{2,1,0:T(4,128)(2,1)} %refs_0_.1, f32[4,2,16,4096]{3,2,1,0:T(8,128)} %bitcast.6, bf16[128,4096]{1,0:T(8,128)(2,1)} %refs_2_.1, bf16[32,4,128,128]{3,2,1,0:T(8,128)(2,1)} %refs_3_.1, f32[1,4096]{1,0:T(1,128)} %bitcast.7, f32[1,4096]{1,0:T(1,128)} %bitcast.8, ...), custom_call_target="tpu_custom_call" | custom-call | tf_op jit(solution)/shard_map/pallas_call | solution.py:638
  57.0 1.0 %shard_map.123 = (bf16[32,4,4096]{2,1,0:T(4,128)(2,1)}, f32[40,128]{1,0:T(8,128)}) custom-call(bf16[32,4,4096]{2,1,0:T(4,128)(2,1)S(1)} %get-tuple-element.4.updated, f32[40,128]{1,0:T(8,128)S(1)} %get-tuple-element.5.gradient), custom_call_target="tpu_custom_call" | custom-call | tf_op jit(solution)/shard_map/pallas_call | solution.py:707

commit v4 on v3

--- a/solution.py
+++ b/solution.py
@@ -12,9 +12,12 @@
 ZONE_DEV = 40
 ROWS = 16
 PARTS = 4
-MAJOR = ()
+LAST = (0, 0)
+HOLD = 1
+PREF = 1
+DEFER = 1
+DYN = 1
 ORDER = [3, 2, 1]
-BACK = [2, 1, 3]
 SLICES = 4
 EARLY = 0
 LAG = 0
@@ -314,7 +317,14 @@
                 halo(piece_of(d), c, p, side, mine=d == 0).start()
 
     order = ORDER if n_harm == 4 else list(range(1, n_harm))
-    back_order = BACK if n_harm == 4 else list(range(1, n_harm))
+    if DYN and n_harm == 4:
+        order = [jnp.int32(2), jnp.where(low, 3, 1), jnp.where(low, 1, 3)]
+    back_order = order
+    if PREF and n_harm == 4:
+        odd = me_h % 2
+        back_order = [2 - odd, 3 - odd, 1 + 2 * odd]
+        if PREF == 2:
+            back_order = [2 - odd, 1 + 2 * odd, 3 - odd]
 
     def send(c):
         for side in range(2):
@@ -324,14 +334,16 @@
                 for p in range(PARTS):
                     depart(c, p, side).start()
 
-        if c in MAJOR:
-            for d in order:
-                for p in range(PARTS):
-                    arrive(d, c, p).start()
+        if LAST[c] == 3:
+            for p in range(PARTS):
+                arrive(order[-1], c, p).start()
         for p in range(PARTS):
-            if c not in MAJOR:
-                for d in order:
-                    arrive(d, c, p).start()
+            for d in order if LAST[c] < 2 else order[:-1]:
+                arrive(d, c, p).start()
+        if LAST[c] == 2:
+            for p in range(PARTS):
+                arrive(order[-1], c, p).start()
+        for p in range(PARTS):
             start_halo(0, c, p)
             for t in range(n_harm - 1):
                 for side in range(2):
@@ -448,9 +460,21 @@
             return carry
 
         lax.fori_loop(0, per_part, block_step, 0, unroll=2)
-        for d in back_order:
-            back(d, c, p).start()
+        if c < n_chunk - 1 or p < PARTS - HOLD:
+            give(c, p)
+
+    def give(c, p):
         own_back(c, p).start()
+        back(back_order[0], c, p).start()
+        if c < n_chunk - 1 or DEFER == 0:
+            for d in back_order[1:]:
+                back(d, c, p).start()
+        else:
+            flush = range(p - DEFER, PARTS if p == PARTS - 1 else p - DEFER + 1)
+            for late in flush:
+                if late >= 0:
+                    for d in back_order[1:]:
+                        back(d, c, late).start()
 
     def wait_halo(c):
         for side in range(2):
@@ -524,14 +548,18 @@
         def _(side=side):
             hand_over(side).start()
 
+    for p in range(PARTS - HOLD, PARTS):
+        give(n_chunk - 1, p)
+
     grad[...] = part[ZONE_DEV : 2 * ZONE_DEV, :]
 
-    for side, buffer in ((0, from_next), (1, from_prev)):
-
-        @pl.when(sides[1 - side][0])
-        def _(side=side, buffer=buffer):
-            hand_over(side).wait_recv()
-            grad[...] += buffer[...]
+    def join():
+        for side, buffer in ((0, from_next), (1, from_prev)):
+
+            @pl.when(sides[1 - side][0])
+            def _(side=side, buffer=buffer):
+                hand_over(side).wait_recv()
+                grad[...] += buffer[...]
 
     def gather(c, p):
         def step(i, carry):
@@ -557,6 +585,8 @@
             for d in range(1, n_harm):
                 back(d, c, p).wait_recv()
             gather(c, p)
+            if c == n_chunk - 1 and p == PARTS - 2:
+                join()
 
     for c in range(n_chunk):
         for p in range(PARTS):

time: 58.1 us -> 57.5 us (0.990)
  the two profiles are of different devices: /device:TPU:16 before, /device:TPU:0 now
where the time goes in v4:
time: 57.5 us; the launch traced here: 57.4 us
  Pallas kernels  56.7 us (99%)
  between operations  0.64 us (1%)
    pallas_call x1, Pallas kernels, body(): pl.pallas_call(functools.partial(kernel, n_harm, n_node, n_chunk), out_sh...  55.7 us

profile of v4, /device:TPU:0, one launch (start us, length us, event | category | flops | bytes accessed | tf_op | source)
XLA Modules:
  0.0 57.4 jit_solution(3629185439475567224)
XLA Ops:
  0.6 55.7 %shard_map.122 = (bf16[32,4,4096]{2,1,0:T(4,128)(2,1)S(1)}, f32[40,128]{1,0:T(8,128)S(1)}) custom-call(bf16[32,4,4096]{2,1,0:T(4,128)(2,1)} %refs_0_.1, f32[4,2,16,4096]{3,2,1,0:T(8,128)} %bitcast.6, bf16[128,4096]{1,0:T(8,128)(2,1)} %refs_2_.1, bf16[32,4,128,128]{3,2,1,0:T(8,128)(2,1)} %refs_3_.1, f32[1,4096]{1,0:T(1,128)} %bitcast.7, f32[1,4096]{1,0:T(1,128)} %bitcast.8, ...), custom_call_target="tpu_custom_call" | custom-call | tf_op jit(solution)/shard_map/pallas_call | solution.py:668
  56.3 1.0 %shard_map.123 = (bf16[32,4,4096]{2,1,0:T(4,128)(2,1)}, f32[40,128]{1,0:T(8,128)}) custom-call(bf16[32,4,4096]{2,1,0:T(4,128)(2,1)S(1)} %get-tuple-element.4.updated, f32[40,128]{1,0:T(8,128)S(1)} %get-tuple-element.5.gradient), custom_call_target="tpu_custom_call" | custom-call | tf_op jit(solution)/shard_map/pallas_call | solution.py:737

commit v5 on v4

--- a/solution.py
+++ b/solution.py
@@ -12,10 +12,10 @@
 ZONE_DEV = 40
 ROWS = 16
 PARTS = 4
-LAST = (0, 0)
+LAST = (3, 3)
 HOLD = 1
 PREF = 1
-DEFER = 1
+DEFER = 2
 DYN = 1
 ORDER = [3, 2, 1]
 SLICES = 4

time: 57.5 us -> 56.4 us (0.981)
  Pallas kernels: 56.7 us -> 55.6 us
    pallas_call x1, Pallas kernels: 55.7 us -> 54.6 us  [body(): pl.pallas_call(functools.partial(kernel, n_harm, n_node, n_chunk), out_sh...]
where the time goes in v5:
time: 56.4 us; the launch traced here: 56.2 us
  Pallas kernels  55.6 us (99%)
  between operations  0.64 us (1%)
    pallas_call x1, Pallas kernels, body(): pl.pallas_call(functools.partial(kernel, n_harm, n_node, n_chunk), out_sh...  54.6 us

profile of v5, /device:TPU:0, one launch (start us, length us, event | category | flops | bytes accessed | tf_op | source)
XLA Modules:
  0.0 56.2 jit_solution(10601814511372834199)
XLA Ops:
  0.6 54.6 %shard_map.122 = (bf16[32,4,4096]{2,1,0:T(4,128)(2,1)S(1)}, f32[40,128]{1,0:T(8,128)S(1)}) custom-call(bf16[32,4,4096]{2,1,0:T(4,128)(2,1)} %refs_0_.1, f32[4,2,16,4096]{3,2,1,0:T(8,128)} %bitcast.6, bf16[128,4096]{1,0:T(8,128)(2,1)} %refs_2_.1, bf16[32,4,128,128]{3,2,1,0:T(8,128)(2,1)} %refs_3_.1, f32[1,4096]{1,0:T(1,128)} %bitcast.7, f32[1,4096]{1,0:T(1,128)} %bitcast.8, ...), custom_call_target="tpu_custom_call" | custom-call | tf_op jit(solution)/shard_map/pallas_call | solution.py:668
  55.2 1.0 %shard_map.123 = (bf16[32,4,4096]{2,1,0:T(4,128)(2,1)}, f32[40,128]{1,0:T(8,128)}) custom-call(bf16[32,4,4096]{2,1,0:T(4,128)(2,1)S(1)} %get-tuple-element.4.updated, f32[40,128]{1,0:T(8,128)S(1)} %get-tuple-element.5.gradient), custom_call_target="tpu_custom_call" | custom-call | tf_op jit(solution)/shard_map/pallas_call | solution.py:737
